TPU v7x, 32 devices: a whole 2x2x4 slice. The times are simulated.
32 devices in a mesh: groups: 2 (over x), row: 16 (over z, y, core).
Axes of the slice: x: 2, y: 2, z: 4, core: 2. Of those that a mesh axis runs over, the one named last changes fastest.
Arguments:
- features: bfloat16 [64, 32, 4, 256], P('groups', 'row'), parts along dimension 0, may hold values from -6 to 6
- axial_taps: float32 [31, 256], replicated, may hold values from -1 to 1
- radial_taps: float32 [31, 256], replicated, may hold values from -1 to 1
- conv_bias: float32 [256], replicated, may hold values from -6 to 6
- ln_gain: float32 [256], replicated, may hold values from 0.5 to 1.5
- ln_bias: float32 [256], replicated, may hold values from -3 to 3
- w_in: bfloat16 [1024, 256], P('row'), may hold values from -0.375 to 0.375
- b_in: bfloat16 [1024], P('row'), may hold values from -3 to 3
- w_out: bfloat16 [1024, 256], P('row'), may hold values from -0.1875 to 0.1875
- b_out: float32 [256], replicated, may hold values from -1.75 to 1.75
- layer_scale: float32 [256], replicated, may hold values from 0.5 to 2
Outputs:
- block_out: bfloat16 [64, 32, 4, 256], P('groups', 'row'), parts along dimension 0
There are 2 independent parts, one for each index of `groups`. A program takes and returns all parts, laid end to end along the dimension named above; an argument that names none is the same for every part. Nothing has to cross between parts.
All inputs are finite; a program needn't handle non-finite values.
Results may differ from a plain program's by a relative error of at most 0.01.
Values may be sent and summed in bfloat16 or wider, within the bound.
A program may use at most 64 MiB of HBM per device.

v0:
```python
from functools import partial

import jax
import jax.numpy as jnp
from jax import lax
from jax.sharding import PartitionSpec as P


def shifted_sum(source, tap_table, along_dim):
    half_span = tap_table.shape[0] // 2
    pad_widths = [(0, 0)] * source.ndim
    pad_widths[along_dim] = (half_span, half_span)
    padded = jnp.pad(source, pad_widths)
    extent = source.shape[along_dim]
    total_sum = jnp.zeros(source.shape, jnp.float32)
    for offset in range(tap_table.shape[0]):
        window = lax.slice_in_dim(padded, offset, offset + extent, axis=along_dim)
        total_sum = total_sum + window.astype(jnp.float32) * tap_table[offset]
    return total_sum


def block_mlp(params, row_block):
    w_in, b_in, w_out, ln_gain, ln_bias, b_out, layer_scale = params
    values = row_block.astype(jnp.float32)
    average = jnp.mean(values, axis=-1, keepdims=True)
    centred = values - average
    variance = jnp.mean(centred * centred, axis=-1, keepdims=True)
    normed = (centred * lax.rsqrt(variance + 1e-06) * ln_gain + ln_bias).astype(jnp.bfloat16)
    pre_act = lax.dot_general(
        normed, w_in, (((1,), (1,)), ((), ())), preferred_element_type=jnp.float32
    )
    pre_act = pre_act + b_in.astype(jnp.float32)
    hidden = jax.nn.gelu(pre_act, approximate=True).astype(jnp.bfloat16)
    projected = jnp.dot(hidden, w_out, preferred_element_type=jnp.float32) + b_out
    return (layer_scale * projected).astype(jnp.bfloat16)


def local(
    features,
    axial_taps,
    radial_taps,
    conv_bias,
    ln_gain,
    ln_bias,
    w_in,
    b_in,
    w_out,
    b_out,
    layer_scale,
):
    w_in_full, b_in_full, w_out_full = (
        lax.all_gather(w_in, "row", axis=0, tiled=True),
        lax.all_gather(b_in, "row", axis=0, tiled=True),
        lax.all_gather(w_out, "row", axis=0, tiled=True),
    )
    params = (w_in_full, b_in_full, w_out_full, ln_gain, ln_bias, b_out, layer_scale)
    channels = features.shape[-1]
    axial_mixed = shifted_sum(features, axial_taps, 0).astype(jnp.bfloat16)
    line_result = (
        shifted_sum(
            lax.all_to_all(axial_mixed, "row", split_axis=0, concat_axis=1, tiled=True),
            radial_taps,
            1,
        )
        + conv_bias
    ).astype(jnp.bfloat16)
    returned = lax.all_to_all(line_result, "row", split_axis=1, concat_axis=0, tiled=True)
    dims_out = returned.shape
    flat_rows = returned.reshape(-1, channels)
    row_count = flat_rows.shape[0]
    block_rows = 1024 if row_count % 1024 == 0 else row_count
    blocked = flat_rows.reshape(row_count // block_rows, block_rows, channels)
    result = lax.map(partial(block_mlp, params), blocked)
    branch = result.reshape(dims_out)
    return (features.astype(jnp.float32) + branch.astype(jnp.float32)).astype(jnp.bfloat16)


def solution(mesh):
    in_specs = (
        P("groups", "row", None, None),
        P(),
        P(),
        P(),
        P(),
        P(),
        P("row", None),
        P("row"),
        P("row", None),
        P(),
        P(),
    )
    out_specs = P("groups", "row", None, None)
    return jax.shard_map(local, mesh=mesh, in_specs=in_specs, out_specs=out_specs, check_vma=False)
```

profile of v0, /device:TPU:1, one launch (start us, length us, event | category | flops | bytes accessed | tf_op | source)
XLA Modules:
  0.0 100.1 jit_solution(3787928823563984789)
XLA Ops:
  0.0 1.0 fusion.45
  1.0 1.0 %fusion.44 = (f32[1,256]{1,0:T(1,128)S(1)}, f32[1,256]{1,0:T(1,128)S(1)}, f32[1,256]{1,0:T(1,128)S(1)}, f32[1,256]{1,0:T(1,128)S(1)}, f32[1,256]{1,0:T(1,128)S(1...) fusion(f32[31,256]{1,0:T(8,128)} %param.12), kind=kLoop, calls=%fused_computation.112 | loop fusion | bytes 38912 | tf_op jit(solution)/shard_map/slice | solution.py:18
  2.0 2.7 %add_convert_fusion.2 = bf16[32,2,4,256]{3,2,1,0:T(4,128)(2,1)} fusion(bf16[32,2,4,256]{3,2,1,0:T(4,128)(2,1)S(1)} %copy-done, f32[256]{0:T(256)S(1)} %bitcast.122, f32[256]{0:T(256)S(1)} %bitcast.123, f32[256]{0:T(256)S(1)} %bitcast.125, f32[256]{0:T(256)S(1)} %bitcast.126, f32[256]{0:T(256)S(1)} %bitcast.127, f32[256]{0:T(256)S(1)} %bitcast.128, ...), kind=kLoop, calls=%fused_computation.98 | loop fusion | flops 6094848 | bytes 293888 | tf_op jit(solution)/shard_map/convert_element_type | solution.py:58
  4.7 7.5 %all-to-all-start = ((bf16[32,2,4,256]{3,2,1,0:T(4,128)(2,1)}), bf16[32,2,4,256]{3,2,1,0:T(4,128)(2,1)S(1)}, u32[]{:S(2)}, u32[]{:S(2)}) async-start(bf16[32,2,4,256]{3,2,1,0:T(4,128)(2,1)} %add_convert_fusion.2), calls=%async_computation | async-start | bytes 262144 | tf_op jit(solution)/shard_map/all_to_all | solution.py:61
  12.3 0.6 copy-done.10
  12.9 0.6 dynamic-slice
  14.2 0.6 copy-done.9
  14.8 0.2 dynamic-update-slice
  15.0 29.3 %all-reduce.2 = bf16[1024]{0:T(1024)(128)(2,1)S(1)} all-reduce(bf16[1024]{0:T(1024)(128)(2,1)S(1)} %dynamic-update-slice), channel_id=1, replica_groups=mesh['groups'=2,'row'=16] {'row'}, use_global_device_ids=true, to_apply=%add.2 | all-reduce | flops 1024 | bytes 4096
  44.2 23.2 %all_gather.9 = bf16[1024,256]{1,0:T(8,128)(2,1)S(1)} all-gather(bf16[64,256]{1,0:T(8,128)(2,1)S(1)} %copy-done.1), channel_id=1, replica_groups=mesh['groups'=2,'row'=16] {'row'}, dimensions={0}, use_global_device_ids=true | all-gather | bytes 557056 | tf_op jit(solution)/shard_map/all_gather | solution.py:52
  67.6 0.7 copy-done.4
  68.3 1.0 add_convert_fusion.1
  69.2 0.8 copy.20
  70.0 4.0 %all-to-all-start.1 = ((bf16[2,32,4,256]{3,2,0,1:T(4,128)(2,1)}), bf16[2,32,4,256]{3,2,0,1:T(4,128)(2,1)S(1)}, u32[]{:S(2)}, u32[]{:S(2)}) async-start(bf16[2,32,4,256]{3,2,0,1:T(4,128)(2,1)} %copy.20), calls=%async_computation.1 | async-start | bytes 262144 | tf_op jit(solution)/shard_map/all_to_all | solution.py:67
  74.0 23.1 %all_gather.11 = bf16[1024,256]{1,0:T(8,128)(2,1)S(1)} all-gather(bf16[64,256]{1,0:T(8,128)(2,1)S(1)} %copy-done.2), channel_id=1, replica_groups=mesh['groups'=2,'row'=16] {'row'}, dimensions={0}, use_global_device_ids=true | all-gather | bytes 557056 | tf_op jit(solution)/shard_map/all_gather | solution.py:54
  97.1 0.2 fusion.41
  97.3 0.3 multiply_reduce_fusion
  97.6 0.1 div.11
  97.8 0.1 rsqrt.13
  97.9 0.1 reshape.112
  98.0 0.5 copy-done.5
  98.6 0.7 fusion.2
  99.3 0.1 reshape.113
  99.4 0.7 fusion.28
  (30 shorter events, 0.3 us)
Async XLA Ops:
  0.0 2.0 %copy-start = (bf16[32,2,4,256]{3,2,1,0:T(4,128)(2,1)S(1)}, bf16[32,2,4,256]{3,2,1,0:T(4,128)(2,1)}, u32[]{:S(2)}) copy-start(bf16[32,2,4,256]{3,2,1,0:T(4,128)(2,1)} %param.11) | copy-start | bytes 393220
  4.7 7.5 %copy-start.3 = (f32[31,256]{1,0:T(8,128)S(1)}, f32[31,256]{1,0:T(8,128)}, u32[]{:S(2)}) copy-start(f32[31,256]{1,0:T(8,128)} %param.13) | copy-start | bytes 95236
  4.7 62.8 %all-to-all-start = ((bf16[32,2,4,256]{3,2,1,0:T(4,128)(2,1)}), bf16[32,2,4,256]{3,2,1,0:T(4,128)(2,1)S(1)}, u32[]{:S(2)}, u32[]{:S(2)}) async-start(bf16[32,2,4,256]{3,2,1,0:T(4,128)(2,1)} %add_convert_fusion.2), calls=%async_computation | async-start | bytes 262144 | tf_op jit(solution)/shard_map/all_to_all | solution.py:61
  12.2 32.1 %copy-start.1 = (bf16[64,256]{1,0:T(8,128)(2,1)S(1)}, bf16[64,256]{1,0:T(8,128)(2,1)}, u32[]{:S(2)}) copy-start(bf16[64,256]{1,0:T(8,128)(2,1)} %param.17) | copy-start | bytes 98308
  12.2 0.7 copy-start.10
  14.1 0.7 copy-start.9
  67.6 0.7 copy-start.4
  70.0 4.0 %copy-start.2 = (bf16[64,256]{1,0:T(8,128)(2,1)S(1)}, bf16[64,256]{1,0:T(8,128)(2,1)}, u32[]{:S(2)}) copy-start(bf16[64,256]{1,0:T(8,128)(2,1)} %param.19) | copy-start | bytes 98308
  70.0 27.1 %all-to-all-start.1 = ((bf16[2,32,4,256]{3,2,0,1:T(4,128)(2,1)}), bf16[2,32,4,256]{3,2,0,1:T(4,128)(2,1)S(1)}, u32[]{:S(2)}, u32[]{:S(2)}) async-start(bf16[2,32,4,256]{3,2,0,1:T(4,128)(2,1)} %copy.20), calls=%async_computation.1 | async-start | bytes 262144 | tf_op jit(solution)/shard_map/all_to_all | solution.py:67
  97.9 0.7 copy-start.5
  97.9 0.7 copy-start.6
  97.9 0.7 copy-start.7
  97.9 0.7 copy-start.8
where the time goes:
time: 101 us; the launch traced here: 100 us
  blocking collectives  75.6 us (75%)
  starting transfers between devices  11.5 us (11%)
  local copies, waits for them, and re-layouts  6.6 us (7%)
  other arithmetic  4.9 us (5%)
    unnamed x1, blocking collectives  29.3 us
    all_gather x1, blocking collectives, local(): lax.all_gather(w_in, 'row', axis=0, tiled=True)  23.2 us
    all_gather x1, blocking collectives, local(): lax.all_gather(w_out, 'row', axis=0, tiled=True)  23.1 us
    all_to_all x1, starting transfers between devices, local(): lax.all_to_all(axial_mixed, 'row', split_axis=0, concat_axis=1, tiled=True)  7.48 us
    all_to_all x1, starting transfers between devices, local(): lax.all_to_all(line_result, 'row', split_axis=1, concat_axis=0, tiled=True)  4 us
    unnamed x25, local copies, waits for them, and re-layouts  3.36 us
    convert_element_type x1, other arithmetic, local(): axial_mixed = shifted_sum(features, axial_taps, 0).astype(jnp.bfloat16)  2.67 us
    slice x4, local copies, waits for them, and re-layouts, shifted_sum(): total_sum = total_sum + window.astype(jnp.float32) * tap_table[offset]  2.02 us
  transfers between devices with their start and end apart: 2, of which 0 were waited for; matrix products, arithmetic and copies ran while one was open for 1% of the time, Pallas kernels for 0%

commit v1 on v0

v1 whole, which is shorter than its diff:
```python
import functools

import jax
import jax.numpy as jnp
from jax import lax
from jax.experimental import pallas as pl
from jax.experimental.pallas import tpu as pltpu
from jax.sharding import PartitionSpec as P

MESH_ID = pl.DeviceIdType.MESH
F32 = jnp.float32
BF16 = jnp.bfloat16


def kernel(
    n, taps, al, hl,
    x_ref, at_ref, rt_ref, cb_ref, lg_ref, lb_ref, wi_ref, bi_ref, wo_ref, bo_ref, ls_ref,
    o_ref,
    xpad, even, odd, send1, recv1, send2, recv2, wts, normed,
    s1_sem, r1_sem, s2_sem, r2_sem, ws_sem, wr_sem,
):
    channels = x_ref.shape[1]
    axial = x_ref.shape[0] // 8
    half = taps // 2
    per = channels // hl
    chips = n // 2
    me = lax.axis_index("row")
    grp = lax.axis_index("groups")
    core = lax.rem(me, 2)
    my_chip = lax.div(me, 2)
    sibling = me + 1 - 2 * core
    my_slot = core * chips + my_chip
    base = core * chips
    other = (1 - core) * chips

    def to(d):
        return (grp, d)

    def ring(i, size, start):
        d = start + i
        return jnp.where(d >= size, d - size, d)

    barrier = pltpu.get_barrier_semaphore()

    def greet(i, c):
        pl.semaphore_signal(barrier, inc=1, device_id=to(ring(i, n, me)), device_id_type=MESH_ID)
        return c

    lax.fori_loop(1, n, greet, 0)

    wts[my_slot, 0:hl, :] = wi_ref[...]
    wts[my_slot, hl : 2 * hl, :] = wo_ref[...]
    unit = lax.broadcasted_iota(jnp.int32, (hl, channels), 0)
    lane = lax.broadcasted_iota(jnp.int32, (hl, channels), 1)
    place = (lane == unit + lax.rem(my_slot, per) * hl).astype(F32).astype(BF16)
    bias16 = jnp.broadcast_to(bi_ref[...].astype(F32), (16, hl)).astype(BF16)
    wts[my_slot, 2 * hl : 2 * hl + 16, :] = jnp.dot(
        bias16, place, preferred_element_type=F32
    ).astype(BF16)

    xpad[0:half] = jnp.zeros((half, 8, channels), F32)
    xpad[axial + half : axial + 2 * half] = jnp.zeros((half, 8, channels), F32)
    zeros8 = jnp.zeros((8, al, 8, channels), F32)
    even[0:8] = zeros8
    even[n + 8 : n + 16] = zeros8
    odd[0:8] = zeros8
    odd[n + 7 : n + 15] = zeros8
    odd[n + 15] = zeros8[0]

    def widen(i, c):
        rows = x_ref[pl.ds(pl.multiple_of(i * 64, 64), 64), :].astype(F32)
        xpad[pl.ds(half + i * 8, 8)] = rows.reshape(8, 8, channels)
        return c

    lax.fori_loop(0, axial // 8, widen, 0)

    def axial_chunk(i, c):
        acc = jnp.zeros((8, 8, channels), F32)
        for k in range(taps):
            acc = acc + xpad[pl.ds(i * 8 + k, 8)] * at_ref[k : k + 1, :][None]
        send1[pl.ds(i * 4, 4)] = acc.reshape(4, 16, channels).astype(BF16)
        return c

    lax.fori_loop(0, axial // 8, axial_chunk, 0)

    pl.semaphore_wait(barrier, n - 1)

    def exchange1(i, c):
        d = ring(i, n, me)
        pltpu.make_async_remote_copy(
            src_ref=send1.at[d], dst_ref=recv1.at[me], send_sem=s1_sem, recv_sem=r1_sem,
            device_id=to(d), device_id_type=MESH_ID,
        ).start()
        return c

    lax.fori_loop(1, n, exchange1, 0)

    def weight_copy(slot, d):
        return pltpu.make_async_remote_copy(
            src_ref=wts.at[slot], dst_ref=wts.at[slot], send_sem=ws_sem, recv_sem=wr_sem.at[slot],
            device_id=to(d), device_id_type=MESH_ID,
        )

    weight_copy(my_slot, sibling).start()

    def gather(i, c):
        weight_copy(my_slot, 2 * ring(i, chips, my_chip) + core).start()
        return c

    lax.fori_loop(1, chips, gather, 0)

    recv1[me] = send1[me]
    arrived = recv1.at[pl.ds(0, n - 1)]
    pltpu.make_async_copy(arrived, arrived, r1_sem).wait()

    def pairs(s, c):
        v = recv1[s].astype(F32).reshape(al, 8, channels)
        even[s + 8] = v
        for a in range(al):
            odd[s + 8, a, 0:4, :] = v[a, 4:8]
            odd[s + 7, a, 4:8, :] = v[a, 0:4]
        return c

    lax.fori_loop(0, n, pairs, 0)

    def radial_chunk(i, c):
        p = i * 4
        acc = jnp.zeros((4, al, 8, channels), F32)
        for k in range(taps):
            shift = k - half
            if shift % 2 == 0:
                window = even[pl.ds(p + 8 + shift // 2, 4)]
            else:
                window = odd[pl.ds(p + 8 + (shift - 1) // 2, 4)]
            acc = acc + window * rt_ref[k : k + 1, :][None, None]
        acc = acc + cb_ref[...][None, None]
        send2[pl.ds(p, 4)] = acc.reshape(4, al * 8, channels).astype(BF16)
        return c

    lax.fori_loop(0, n // 4, radial_chunk, 0)

    def exchange2(i, c):
        d = ring(i, n, me)
        pltpu.make_async_remote_copy(
            src_ref=send2.at[d], dst_ref=recv2.at[me], send_sem=s2_sem, recv_sem=r2_sem,
            device_id=to(d), device_id_type=MESH_ID,
        ).start()
        return c

    lax.fori_loop(1, n, exchange2, 0)
    recv2[me] = send2[me]

    def forward(i, c):
        slot = base + ring(chips - i, chips, my_chip)
        weight_copy(slot, sibling).wait_recv()
        weight_copy(slot, sibling).start()
        return c

    lax.fori_loop(1, chips, forward, 0)

    arrived2 = recv2.at[pl.ds(0, n - 1)]
    pltpu.make_async_copy(arrived2, arrived2, r2_sem).wait()

    block = min(16, n)
    rows = block * 16

    def norm(b, c):
        v = recv2[pl.ds(b * block, block)].reshape(rows, channels).astype(F32)
        average = jnp.mean(v, axis=-1, keepdims=True)
        centred = v - average
        variance = jnp.mean(centred * centred, axis=-1, keepdims=True)
        z = centred * lax.rsqrt(variance + 1e-06) * lg_ref[...] + lb_ref[...]
        normed[pl.ds(pl.multiple_of(b * rows, rows), rows), :] = z.astype(BF16)
        return c

    lax.fori_loop(0, n // block, norm, 0)

    def flat(w):
        if hl % 16:
            return w.astype(F32).reshape(per * hl, channels).astype(BF16)
        return w.reshape(per * hl, channels)

    def project(z, first):
        w_in = flat(wts[pl.ds(first, per), 0:hl, :])
        w_out = flat(wts[pl.ds(first, per), hl : 2 * hl, :])
        b_in = jnp.sum(wts[pl.ds(first, per), 2 * hl : 2 * hl + 16, :].astype(F32), axis=0)[0:1]
        u = lax.dot_general(z, w_in, (((1,), (1,)), ((), ())), preferred_element_type=F32) + b_in
        g = 0.5 * u * (1.0 + jnp.tanh(0.7978845608028654 * (u + 0.044715 * (u * u * u))))
        return jnp.dot(g.astype(BF16), w_out, preferred_element_type=F32)

    def others(i, c):
        weight_copy(other + i, sibling).wait_recv()
        return c

    def mlp(b, c, late):
        at = pl.ds(pl.multiple_of(b * rows, rows), rows)
        z = normed[at, :]
        total = project(z, base)
        for g in range(1, chips // per):
            total = total + project(z, base + g * per)
        if late:
            lax.fori_loop(0, chips, others, 0)
        for g in range(chips // per):
            total = total + project(z, other + g * per)
        branch = (ls_ref[...] * (total + bo_ref[...])).astype(BF16)
        o_ref[at, :] = (x_ref[at, :].astype(F32) + branch.astype(F32)).astype(BF16)
        return c

    mlp(0, 0, True)
    if n // block > 1:
        lax.fori_loop(1, n // block, lambda b, c: mlp(b, c, False), 0)

    sent = send1.at[pl.ds(0, n - 1)]
    pltpu.make_async_copy(sent, sent, s1_sem).wait()
    sent2 = send2.at[pl.ds(0, n - 1)]
    pltpu.make_async_copy(sent2, sent2, s2_sem).wait()
    passed = wts.at[pl.ds(0, n - 1)]
    pltpu.make_async_copy(passed, passed, ws_sem).wait()


def local(
    features,
    axial_taps,
    radial_taps,
    conv_bias,
    ln_gain,
    ln_bias,
    w_in,
    b_in,
    w_out,
    b_out,
    layer_scale,
    n,
):
    axial, radial, theta, channels = features.shape
    taps = axial_taps.shape[0]
    hl = w_in.shape[0]
    al = axial // n
    assert radial * theta == 8 and al == 2 and channels == 256 and taps == 31
    flat = features.reshape(axial * 8, channels)

    def row(v):
        return v.reshape(1, -1)

    vmem = pl.BlockSpec(memory_space=pltpu.VMEM)
    dma = pltpu.SemaphoreType.DMA
    out = pl.pallas_call(
        functools.partial(kernel, n, taps, al, hl),
        out_shape=jax.ShapeDtypeStruct(flat.shape, BF16),
        in_specs=[vmem] * 11,
        out_specs=vmem,
        scratch_shapes=[
            pltpu.VMEM((axial + taps - 1, 8, channels), F32),
            pltpu.VMEM((n + 16, al, 8, channels), F32),
            pltpu.VMEM((n + 16, al, 8, channels), F32),
            pltpu.VMEM((n, 16, channels), BF16),
            pltpu.VMEM((n, 16, channels), BF16),
            pltpu.VMEM((n, 16, channels), BF16),
            pltpu.VMEM((n, 16, channels), BF16),
            pltpu.VMEM((n, 2 * hl + 16, channels), BF16),
            pltpu.VMEM((axial * 8, channels), BF16),
            dma, dma, dma, dma, dma,
            dma((n,)),
        ],
        compiler_params=pltpu.CompilerParams(
            collective_id=0, has_side_effects=True, vmem_limit_bytes=40 * 1024 * 1024
        ),
        cost_estimate=pl.CostEstimate(
            flops=axial * 8 * channels * 4 * (n * hl + taps),
            bytes_accessed=4 * axial * 8 * channels + 4 * n * hl * channels,
            transcendentals=axial * 8 * n * hl,
        ),
    )(
        flat, axial_taps, radial_taps, row(conv_bias), row(ln_gain), row(ln_bias),
        w_in, row(b_in), w_out, row(b_out), row(layer_scale),
    )
    return out.reshape(features.shape)


def solution(mesh):
    in_specs = (
        P("groups", "row", None, None),
        P(),
        P(),
        P(),
        P(),
        P(),
        P("row", None),
        P("row"),
        P("row", None),
        P(),
        P(),
    )
    out_specs = P("groups", "row", None, None)
    body = functools.partial(local, n=mesh.shape["row"])
    return jax.shard_map(body, mesh=mesh, in_specs=in_specs, out_specs=out_specs, check_vma=False)
```

time: 101 us -> 28.2 us (0.28)
  blocking collectives: 75.6 us -> 0 us
  Pallas kernels: 0 us -> 25.9 us
  starting transfers between devices: 11.5 us -> 0 us
  other arithmetic: 4.9 us -> 0 us
  local copies, waits for them, and re-layouts: 6.6 us -> 1.75 us
    all_gather x2 -> x0, blocking collectives: 46.3 us -> none  [the longest x1 23.2 us: local(): lax.all_gather(w_in, 'row', axis=0, tiled=True)]
    unnamed x1 -> x0, blocking collectives: 29.3 us -> none
    pallas_call x0 -> x1, Pallas kernels: none -> 25.9 us  [local(): pl.pallas_call(functools.partial(kernel, n, taps, al, hl), out_shape=jax....]
    all_to_all x2 -> x0, starting transfers between devices: 11.5 us -> none  [the longest x1 7.48 us: local(): lax.all_to_all(axial_mixed, 'row', split_axis=0, concat_axis=1, tiled=True)]
    convert_element_type x6 -> x0, other arithmetic: 4.4 us -> none  [the longest x1 2.67 us: local(): axial_mixed = shifted_sum(features, axial_taps, 0).astype(jnp.bfloat16)]
    unnamed x25 -> x20, local copies, waits for them, and re-layouts: 3.36 us -> 0.04 us
    slice x4 -> x0, local copies, waits for them, and re-layouts: 2.02 us -> none  [shifted_sum(): total_sum = total_sum + window.astype(jnp.float32) * tap_table[offset]]
    reshape x0 -> x2, local copies, waits for them, and re-layouts: none -> 1.71 us  [the longest x1 1.02 us: local(): flat = features.reshape(axial * 8, channels)]
  transfers between devices with their start and end apart: 2 -> 0, of which waited for: 0 -> 0; matrix products, arithmetic and copies ran while one was open for 1% -> 0% of each run, Pallas kernels for 0% -> 0%
where the time goes in v1:
time: 28.2 us; the launch traced here: 27.8 us
  Pallas kernels  25.9 us (92%)
  local copies, waits for them, and re-layouts  1.75 us (6%)
    pallas_call x1, Pallas kernels, local(): pl.pallas_call(functools.partial(kernel, n, taps, al, hl), out_shape=jax....  25.9 us
    reshape x1, local copies, waits for them, and re-layouts, local(): flat = features.reshape(axial * 8, channels)  1.02 us
    reshape x1, local copies, waits for them, and re-layouts, local(): return out.reshape(features.shape)  0.69 us

profile of v1, /device:TPU:1, one launch (start us, length us, event | category | flops | bytes accessed | tf_op | source)
XLA Modules:
  0.0 27.8 jit_solution(10990811437792977275)
XLA Ops:
  0.0 0.0 copy-start
  0.0 0.0 copy-start.1
  0.0 0.0 copy-start.2
  0.0 0.0 copy-start.3
  0.0 0.0 copy-start.4
  0.0 0.0 copy-start.5
  0.0 0.0 copy-start.6
  0.0 0.0 copy-start.7
  0.1 0.0 copy-start.8
  0.1 0.0 copy-start.9
  0.1 1.0 %reshape.24.x_ref = bf16[256,256]{1,0:T(8,128)(2,1)S(1)} reshape(bf16[32,2,4,256]{3,2,1,0:T(4,128)(2,1)} %param.11) | data formatting | bytes 262144 | tf_op jit(solution)/shard_map/reshape | solution.py:240
  1.1 0.0 copy-done
  1.1 0.0 copy-done.1
  1.1 0.0 copy-done.2
  1.1 0.0 copy-done.3
  1.1 0.0 copy-done.4
  1.1 0.0 copy-done.5
  1.2 0.0 copy-done.6
  1.2 0.0 copy-done.7
  1.2 0.0 copy-done.8
  1.2 0.0 copy-done.9
  1.2 25.9 %shard_map.109 = bf16[256,256]{1,0:T(8,128)(2,1)S(1)} custom-call(bf16[256,256]{1,0:T(8,128)(2,1)S(1)} %reshape.24.x_ref, f32[31,256]{1,0:T(8,128)S(1)} %copy-done, f32[31,256]{1,0:T(8,128)S(1)} %copy-done.1, f32[1,256]{1,0:T(1,128)S(1)} %bitcast.6, f32[1,256]{1,0:T(1,128)S(1)} %bitcast.7, f32[1,256]{1,0:T(1,128)S(1)} %bitcast.8, ...), custom_call_target="tpu_custom_call" | custom-call | flops 276561920 | bytes 1310720 | tf_op jit(solution)/shard_map/pallas_call | solution.py:247
  27.1 0.7 %reshape.31 = bf16[32,2,4,256]{3,2,1,0:T(4,128)(2,1)} reshape(bf16[256,256]{1,0:T(8,128)(2,1)S(1)} %shard_map.109) | data formatting | bytes 262144 | tf_op jit(solution)/shard_map/reshape | solution.py:277
Async XLA Ops:
  0.0 1.1 %copy-start = (f32[31,256]{1,0:T(8,128)S(1)}, f32[31,256]{1,0:T(8,128)}, u32[]{:S(2)}) copy-start(f32[31,256]{1,0:T(8,128)} %at_ref.1) | copy-start | bytes 95236
  0.0 1.1 %copy-start.1 = (f32[31,256]{1,0:T(8,128)S(1)}, f32[31,256]{1,0:T(8,128)}, u32[]{:S(2)}) copy-start(f32[31,256]{1,0:T(8,128)} %rt_ref.1) | copy-start | bytes 95236
  0.0 1.1 %copy-start.2 = (bf16[64,256]{1,0:T(8,128)(2,1)S(1)}, bf16[64,256]{1,0:T(8,128)(2,1)}, u32[]{:S(2)}) copy-start(bf16[64,256]{1,0:T(8,128)(2,1)} %wi_ref.1) | copy-start | bytes 98308
  0.0 1.1 %copy-start.3 = (bf16[64,256]{1,0:T(8,128)(2,1)S(1)}, bf16[64,256]{1,0:T(8,128)(2,1)}, u32[]{:S(2)}) copy-start(bf16[64,256]{1,0:T(8,128)(2,1)} %wo_ref.1) | copy-start | bytes 98308
  0.0 1.1 %copy-start.4 = (f32[256]{0:T(256)S(1)}, f32[256]{0:T(256)}, u32[]{:S(2)}) copy-start(f32[256]{0:T(256)} %param.14) | copy-start | bytes 3076
  0.0 1.1 %copy-start.5 = (f32[256]{0:T(256)S(1)}, f32[256]{0:T(256)}, u32[]{:S(2)}) copy-start(f32[256]{0:T(256)} %param.15) | copy-start | bytes 3076
  0.0 1.1 %copy-start.6 = (f32[256]{0:T(256)S(1)}, f32[256]{0:T(256)}, u32[]{:S(2)}) copy-start(f32[256]{0:T(256)} %param.16) | copy-start | bytes 3076
  0.0 1.1 %copy-start.7 = (f32[256]{0:T(256)S(1)}, f32[256]{0:T(256)}, u32[]{:S(2)}) copy-start(f32[256]{0:T(256)} %param.20) | copy-start | bytes 3076
  0.1 1.1 %copy-start.8 = (f32[256]{0:T(256)S(1)}, f32[256]{0:T(256)}, u32[]{:S(2)}) copy-start(f32[256]{0:T(256)} %param.21) | copy-start | bytes 3076
  0.1 1.1 %copy-start.9 = (bf16[64]{0:T(256)(128)(2,1)S(1)}, bf16[64]{0:T(256)(128)(2,1)}, u32[]{:S(2)}) copy-start(bf16[64]{0:T(256)(128)(2,1)} %param.18) | copy-start | bytes 388

commit v2 on v1

--- a/solution.py
+++ b/solution.py
@@ -13,11 +13,11 @@
 
 
 def kernel(
-    n, taps, al, hl,
+    n, inner, taps, al, hl,
     x_ref, at_ref, rt_ref, cb_ref, lg_ref, lb_ref, wi_ref, bi_ref, wo_ref, bo_ref, ls_ref,
     o_ref,
-    xpad, even, odd, send1, recv1, send2, recv2, wts, normed,
-    s1_sem, r1_sem, s2_sem, r2_sem, ws_sem, wr_sem,
+    xpad, even, odd, send1, recv1, send2, recv2, wts, bias, normed,
+    s1_sem, r1_sem, s2_sem, r2_sem, ws_sem, bs_sem, br_sem, wr_sem,
 ):
     channels = x_ref.shape[1]
     axial = x_ref.shape[0] // 8
@@ -32,6 +32,9 @@
     my_slot = core * chips + my_chip
     base = core * chips
     other = (1 - core) * chips
+    outer = chips // inner
+    my_z = lax.div(my_chip, inner)
+    my_y = lax.rem(my_chip, inner)
 
     def to(d):
         return (grp, d)
@@ -47,16 +50,15 @@
         return c
 
     lax.fori_loop(1, n, greet, 0)
-
-    wts[my_slot, 0:hl, :] = wi_ref[...]
-    wts[my_slot, hl : 2 * hl, :] = wo_ref[...]
+    pl.semaphore_signal(barrier, inc=1, device_id=(1 - grp, me), device_id_type=MESH_ID)
+
+    wts[my_slot] = wi_ref[...]
+    wts[n + my_slot] = wo_ref[...]
     unit = lax.broadcasted_iota(jnp.int32, (hl, channels), 0)
     lane = lax.broadcasted_iota(jnp.int32, (hl, channels), 1)
     place = (lane == unit + lax.rem(my_slot, per) * hl).astype(F32).astype(BF16)
     bias16 = jnp.broadcast_to(bi_ref[...].astype(F32), (16, hl)).astype(BF16)
-    wts[my_slot, 2 * hl : 2 * hl + 16, :] = jnp.dot(
-        bias16, place, preferred_element_type=F32
-    ).astype(BF16)
+    bias[my_slot] = jnp.dot(bias16, place, preferred_element_type=F32)[0:1]
 
     xpad[0:half] = jnp.zeros((half, 8, channels), F32)
     xpad[axial + half : axial + 2 * half] = jnp.zeros((half, 8, channels), F32)
@@ -83,7 +85,7 @@
 
     lax.fori_loop(0, axial // 8, axial_chunk, 0)
 
-    pl.semaphore_wait(barrier, n - 1)
+    pl.semaphore_wait(barrier, n)
 
     def exchange1(i, c):
         d = ring(i, n, me)
@@ -95,19 +97,42 @@
 
     lax.fori_loop(1, n, exchange1, 0)
 
-    def weight_copy(slot, d):
+    mine = grp * n
+    theirs = (1 - grp) * n
+
+    def piece_copy(piece, g, d):
         return pltpu.make_async_remote_copy(
-            src_ref=wts.at[slot], dst_ref=wts.at[slot], send_sem=ws_sem, recv_sem=wr_sem.at[slot],
+            src_ref=wts.at[piece], dst_ref=wts.at[piece], send_sem=ws_sem,
+            recv_sem=wr_sem.at[piece], device_id=(g, d), device_id_type=MESH_ID,
+        )
+
+    def chip_of(z, y):
+        return z * inner + y
+
+    def to_inner(piece):
+        for j in range(1, inner):
+            y = ring(j, inner, my_y)
+            piece_copy(piece, grp, 2 * chip_of(my_z, y) + core).start()
+
+    def own_outer(i, c):
+        z = ring(i, outer, my_z)
+        piece_copy(mine + my_slot, grp, 2 * chip_of(z, my_y) + core).start()
+        return c
+
+    lax.fori_loop(1, outer, own_outer, 0)
+    to_inner(mine + my_slot)
+    piece_copy(mine + my_slot, grp, sibling).start()
+    piece_copy(theirs + my_slot, grp, sibling).start()
+
+    def send_bias(i, c):
+        d = ring(i, n, me)
+        pltpu.make_async_remote_copy(
+            src_ref=bias.at[my_slot], dst_ref=bias.at[my_slot], send_sem=bs_sem, recv_sem=br_sem,
             device_id=to(d), device_id_type=MESH_ID,
-        )
-
-    weight_copy(my_slot, sibling).start()
-
-    def gather(i, c):
-        weight_copy(my_slot, 2 * ring(i, chips, my_chip) + core).start()
-        return c
-
-    lax.fori_loop(1, chips, gather, 0)
+        ).start()
+        return c
+
+    lax.fori_loop(1, n, send_bias, 0)
 
     recv1[me] = send1[me]
     arrived = recv1.at[pl.ds(0, n - 1)]
@@ -150,14 +175,36 @@
     lax.fori_loop(1, n, exchange2, 0)
     recv2[me] = send2[me]
 
-    def forward(i, c):
-        slot = base + ring(chips - i, chips, my_chip)
-        weight_copy(slot, sibling).wait_recv()
-        weight_copy(slot, sibling).start()
-        return c
-
-    lax.fori_loop(1, chips, forward, 0)
-
+    def from_outer(i, c):
+        piece = mine + base + chip_of(ring(i, outer, my_z), my_y)
+        piece_copy(piece, grp, sibling).wait_recv()
+        to_inner(piece)
+        piece_copy(piece, 1 - grp, me).start()
+        piece_copy(piece, grp, sibling).start()
+        return c
+
+    lax.fori_loop(1, outer, from_outer, 0)
+
+    def from_inner(i, c):
+        for j in range(1, inner):
+            piece = mine + base + chip_of(ring(i, outer, my_z), ring(j, inner, my_y))
+            piece_copy(piece, grp, sibling).wait_recv()
+            piece_copy(piece, 1 - grp, me).start()
+            piece_copy(piece, grp, sibling).start()
+        return c
+
+    lax.fori_loop(0, outer, from_inner, 0)
+
+    def from_group(i, c):
+        piece = theirs + base + ring(i, chips, my_chip)
+        piece_copy(piece, grp, sibling).wait_recv()
+        piece_copy(piece, grp, sibling).start()
+        return c
+
+    lax.fori_loop(1, chips, from_group, 0)
+
+    arrived3 = bias.at[pl.ds(0, n - 1)]
+    pltpu.make_async_copy(arrived3, arrived3, br_sem).wait()
     arrived2 = recv2.at[pl.ds(0, n - 1)]
     pltpu.make_async_copy(arrived2, arrived2, r2_sem).wait()
 
@@ -181,15 +228,16 @@
         return w.reshape(per * hl, channels)
 
     def project(z, first):
-        w_in = flat(wts[pl.ds(first, per), 0:hl, :])
-        w_out = flat(wts[pl.ds(first, per), hl : 2 * hl, :])
-        b_in = jnp.sum(wts[pl.ds(first, per), 2 * hl : 2 * hl + 16, :].astype(F32), axis=0)[0:1]
+        w_in = flat(wts[pl.ds(first, per)])
+        w_out = flat(wts[pl.ds(n + first, per)])
+        b_in = jnp.sum(bias[pl.ds(first, per)], axis=0)
         u = lax.dot_general(z, w_in, (((1,), (1,)), ((), ())), preferred_element_type=F32) + b_in
         g = 0.5 * u * (1.0 + jnp.tanh(0.7978845608028654 * (u + 0.044715 * (u * u * u))))
         return jnp.dot(g.astype(BF16), w_out, preferred_element_type=F32)
 
     def others(i, c):
-        weight_copy(other + i, sibling).wait_recv()
+        piece_copy(other + i, grp, sibling).wait_recv()
+        piece_copy(n + other + i, grp, sibling).wait_recv()
         return c
 
     def mlp(b, c, late):
@@ -214,8 +262,9 @@
     pltpu.make_async_copy(sent, sent, s1_sem).wait()
     sent2 = send2.at[pl.ds(0, n - 1)]
     pltpu.make_async_copy(sent2, sent2, s2_sem).wait()
-    passed = wts.at[pl.ds(0, n - 1)]
+    passed = wts.at[pl.ds(0, 2 * n - 2)]
     pltpu.make_async_copy(passed, passed, ws_sem).wait()
+    pltpu.make_async_copy(arrived3, arrived3, bs_sem).wait()
 
 
 def local(
@@ -231,11 +280,16 @@
     b_out,
     layer_scale,
     n,
+    groups,
 ):
     axial, radial, theta, channels = features.shape
     taps = axial_taps.shape[0]
     hl = w_in.shape[0]
     al = axial // n
+    inner = 1
+    while 4 * inner * inner <= n // 2:
+        inner *= 2
+    assert groups == 2
     assert radial * theta == 8 and al == 2 and channels == 256 and taps == 31
     flat = features.reshape(axial * 8, channels)
 
@@ -245,7 +299,7 @@
     vmem = pl.BlockSpec(memory_space=pltpu.VMEM)
     dma = pltpu.SemaphoreType.DMA
     out = pl.pallas_call(
-        functools.partial(kernel, n, taps, al, hl),
+        functools.partial(kernel, n, inner, taps, al, hl),
         out_shape=jax.ShapeDtypeStruct(flat.shape, BF16),
         in_specs=[vmem] * 11,
         out_specs=vmem,
@@ -257,10 +311,11 @@
             pltpu.VMEM((n, 16, channels), BF16),
             pltpu.VMEM((n, 16, channels), BF16),
             pltpu.VMEM((n, 16, channels), BF16),
-            pltpu.VMEM((n, 2 * hl + 16, channels), BF16),
+            pltpu.VMEM((2 * n, hl, channels), BF16),
+            pltpu.VMEM((n, 1, channels), F32),
             pltpu.VMEM((axial * 8, channels), BF16),
-            dma, dma, dma, dma, dma,
-            dma((n,)),
+            dma, dma, dma, dma, dma, dma, dma,
+            dma((2 * n,)),
         ],
         compiler_params=pltpu.CompilerParams(
             collective_id=0, has_side_effects=True, vmem_limit_bytes=40 * 1024 * 1024
@@ -292,5 +347,5 @@
         P(),
     )
     out_specs = P("groups", "row", None, None)
-    body = functools.partial(local, n=mesh.shape["row"])
+    body = functools.partial(local, n=mesh.shape["row"], groups=mesh.shape["groups"])
     return jax.shard_map(body, mesh=mesh, in_specs=in_specs, out_specs=out_specs, check_vma=False)

time: 28.2 us -> 24.6 us (0.87); the launches traced: 27.8 us -> 24.5 us
  Pallas kernels: 25.9 us -> 22.6 us
    pallas_call x1, Pallas kernels: 25.9 us -> 22.6 us  [local(): pl.pallas_call(functools.partial(kernel, n, inner, taps, al, hl), out_sha...]
where the time goes in v2:
time: 24.6 us; the launch traced here: 24.5 us
  Pallas kernels  22.6 us (92%)
  local copies, waits for them, and re-layouts  1.75 us (7%)
    pallas_call x1, Pallas kernels, local(): pl.pallas_call(functools.partial(kernel, n, inner, taps, al, hl), out_sha...  22.6 us
    reshape x1, local copies, waits for them, and re-layouts, local(): flat = features.reshape(axial * 8, channels)  1.02 us
    reshape x1, local copies, waits for them, and re-layouts, local(): return out.reshape(features.shape)  0.69 us

profile of v2, /device:TPU:1, one launch (start us, length us, event | category | flops | bytes accessed | tf_op | source)
XLA Modules:
  0.0 24.5 jit_solution(9420008443556547335)
XLA Ops:
  0.0 0.0 copy-start
  0.0 0.0 copy-start.1
  0.0 0.0 copy-start.2
  0.0 0.0 copy-start.3
  0.0 0.0 copy-start.4
  0.0 0.0 copy-start.5
  0.0 0.0 copy-start.6
  0.0 0.0 copy-start.7
  0.1 0.0 copy-start.8
  0.1 0.0 copy-start.9
  0.1 1.0 %reshape.24.x_ref = bf16[256,256]{1,0:T(8,128)(2,1)S(1)} reshape(bf16[32,2,4,256]{3,2,1,0:T(4,128)(2,1)} %param.11) | data formatting | bytes 262144 | tf_op jit(solution)/shard_map/reshape | solution.py:294
  1.1 0.0 copy-done
  1.1 0.0 copy-done.1
  1.1 0.0 copy-done.2
  1.1 0.0 copy-done.3
  1.1 0.0 copy-done.4
  1.1 0.0 copy-done.5
  1.2 0.0 copy-done.6
  1.2 0.0 copy-done.7
  1.2 0.0 copy-done.8
  1.2 0.0 copy-done.9
  1.2 22.6 %shard_map.109 = bf16[256,256]{1,0:T(8,128)(2,1)S(1)} custom-call(bf16[256,256]{1,0:T(8,128)(2,1)S(1)} %reshape.24.x_ref, f32[31,256]{1,0:T(8,128)S(1)} %copy-done, f32[31,256]{1,0:T(8,128)S(1)} %copy-done.1, f32[1,256]{1,0:T(1,128)S(1)} %bitcast.6, f32[1,256]{1,0:T(1,128)S(1)} %bitcast.7, f32[1,256]{1,0:T(1,128)S(1)} %bitcast.8, ...), custom_call_target="tpu_custom_call" | custom-call | flops 276561920 | bytes 1310720 | tf_op jit(solution)/shard_map/pallas_call | solution.py:301
  23.8 0.7 %reshape.31 = bf16[32,2,4,256]{3,2,1,0:T(4,128)(2,1)} reshape(bf16[256,256]{1,0:T(8,128)(2,1)S(1)} %shard_map.109) | data formatting | bytes 262144 | tf_op jit(solution)/shard_map/reshape | solution.py:332
Async XLA Ops:
  0.0 1.1 %copy-start = (f32[31,256]{1,0:T(8,128)S(1)}, f32[31,256]{1,0:T(8,128)}, u32[]{:S(2)}) copy-start(f32[31,256]{1,0:T(8,128)} %at_ref.1) | copy-start | bytes 95236
  0.0 1.1 %copy-start.1 = (f32[31,256]{1,0:T(8,128)S(1)}, f32[31,256]{1,0:T(8,128)}, u32[]{:S(2)}) copy-start(f32[31,256]{1,0:T(8,128)} %rt_ref.1) | copy-start | bytes 95236
  0.0 1.1 %copy-start.2 = (bf16[64,256]{1,0:T(8,128)(2,1)S(1)}, bf16[64,256]{1,0:T(8,128)(2,1)}, u32[]{:S(2)}) copy-start(bf16[64,256]{1,0:T(8,128)(2,1)} %wi_ref.1) | copy-start | bytes 98308
  0.0 1.1 %copy-start.3 = (bf16[64,256]{1,0:T(8,128)(2,1)S(1)}, bf16[64,256]{1,0:T(8,128)(2,1)}, u32[]{:S(2)}) copy-start(bf16[64,256]{1,0:T(8,128)(2,1)} %wo_ref.1) | copy-start | bytes 98308
  0.0 1.1 %copy-start.4 = (f32[256]{0:T(256)S(1)}, f32[256]{0:T(256)}, u32[]{:S(2)}) copy-start(f32[256]{0:T(256)} %param.14) | copy-start | bytes 3076
  0.0 1.1 %copy-start.5 = (f32[256]{0:T(256)S(1)}, f32[256]{0:T(256)}, u32[]{:S(2)}) copy-start(f32[256]{0:T(256)} %param.15) | copy-start | bytes 3076
  0.0 1.1 %copy-start.6 = (f32[256]{0:T(256)S(1)}, f32[256]{0:T(256)}, u32[]{:S(2)}) copy-start(f32[256]{0:T(256)} %param.16) | copy-start | bytes 3076
  0.0 1.1 %copy-start.7 = (f32[256]{0:T(256)S(1)}, f32[256]{0:T(256)}, u32[]{:S(2)}) copy-start(f32[256]{0:T(256)} %param.20) | copy-start | bytes 3076
  0.1 1.1 %copy-start.8 = (f32[256]{0:T(256)S(1)}, f32[256]{0:T(256)}, u32[]{:S(2)}) copy-start(f32[256]{0:T(256)} %param.21) | copy-start | bytes 3076
  0.1 1.1 %copy-start.9 = (bf16[64]{0:T(256)(128)(2,1)S(1)}, bf16[64]{0:T(256)(128)(2,1)}, u32[]{:S(2)}) copy-start(bf16[64]{0:T(256)(128)(2,1)} %param.18) | copy-start | bytes 388

commit v3 on v2

--- a/solution.py
+++ b/solution.py
@@ -138,6 +138,16 @@
     arrived = recv1.at[pl.ds(0, n - 1)]
     pltpu.make_async_copy(arrived, arrived, r1_sem).wait()
 
+    def from_outer(i, c):
+        piece = mine + base + chip_of(ring(i, outer, my_z), my_y)
+        piece_copy(piece, grp, sibling).wait_recv()
+        to_inner(piece)
+        piece_copy(piece, 1 - grp, me).start()
+        piece_copy(piece, grp, sibling).start()
+        return c
+
+    lax.fori_loop(1, outer, from_outer, 0)
+
     def pairs(s, c):
         v = recv1[s].astype(F32).reshape(al, 8, channels)
         even[s + 8] = v
@@ -174,16 +184,6 @@
 
     lax.fori_loop(1, n, exchange2, 0)
     recv2[me] = send2[me]
-
-    def from_outer(i, c):
-        piece = mine + base + chip_of(ring(i, outer, my_z), my_y)
-        piece_copy(piece, grp, sibling).wait_recv()
-        to_inner(piece)
-        piece_copy(piece, 1 - grp, me).start()
-        piece_copy(piece, grp, sibling).start()
-        return c
-
-    lax.fori_loop(1, outer, from_outer, 0)
 
     def from_inner(i, c):
         for j in range(1, inner):

time: 24.6 us -> 23.2 us (0.943)
  Pallas kernels: 22.6 us -> 21.2 us
    pallas_call x1, Pallas kernels: 22.6 us -> 21.2 us  [local(): pl.pallas_call(functools.partial(kernel, n, inner, taps, al, hl), out_sha...]
where the time goes in v3:
time: 23.2 us; the launch traced here: 23.1 us
  Pallas kernels  21.2 us (91%)
  local copies, waits for them, and re-layouts  1.75 us (8%)
    pallas_call x1, Pallas kernels, local(): pl.pallas_call(functools.partial(kernel, n, inner, taps, al, hl), out_sha...  21.2 us
    reshape x1, local copies, waits for them, and re-layouts, local(): flat = features.reshape(axial * 8, channels)  1.02 us
    reshape x1, local copies, waits for them, and re-layouts, local(): return out.reshape(features.shape)  0.69 us

profile of v3, /device:TPU:1, one launch (start us, length us, event | category | flops | bytes accessed | tf_op | source)
XLA Modules:
  0.0 23.1 jit_solution(14862056827421057499)
XLA Ops:
  0.0 0.0 copy-start
  0.0 0.0 copy-start.1
  0.0 0.0 copy-start.2
  0.0 0.0 copy-start.3
  0.0 0.0 copy-start.4
  0.0 0.0 copy-start.5
  0.0 0.0 copy-start.6
  0.0 0.0 copy-start.7
  0.1 0.0 copy-start.8
  0.1 0.0 copy-start.9
  0.1 1.0 %reshape.24.x_ref = bf16[256,256]{1,0:T(8,128)(2,1)S(1)} reshape(bf16[32,2,4,256]{3,2,1,0:T(4,128)(2,1)} %param.11) | data formatting | bytes 262144 | tf_op jit(solution)/shard_map/reshape | solution.py:294
  1.1 0.0 copy-done
  1.1 0.0 copy-done.1
  1.1 0.0 copy-done.2
  1.1 0.0 copy-done.3
  1.1 0.0 copy-done.4
  1.1 0.0 copy-done.5
  1.2 0.0 copy-done.6
  1.2 0.0 copy-done.7
  1.2 0.0 copy-done.8
  1.2 0.0 copy-done.9
  1.2 21.2 %shard_map.109 = bf16[256,256]{1,0:T(8,128)(2,1)S(1)} custom-call(bf16[256,256]{1,0:T(8,128)(2,1)S(1)} %reshape.24.x_ref, f32[31,256]{1,0:T(8,128)S(1)} %copy-done, f32[31,256]{1,0:T(8,128)S(1)} %copy-done.1, f32[1,256]{1,0:T(1,128)S(1)} %bitcast.6, f32[1,256]{1,0:T(1,128)S(1)} %bitcast.7, f32[1,256]{1,0:T(1,128)S(1)} %bitcast.8, ...), custom_call_target="tpu_custom_call" | custom-call | flops 276561920 | bytes 1310720 | tf_op jit(solution)/shard_map/pallas_call | solution.py:301
  22.4 0.7 %reshape.31 = bf16[32,2,4,256]{3,2,1,0:T(4,128)(2,1)} reshape(bf16[256,256]{1,0:T(8,128)(2,1)S(1)} %shard_map.109) | data formatting | bytes 262144 | tf_op jit(solution)/shard_map/reshape | solution.py:332
Async XLA Ops:
  0.0 1.1 %copy-start = (f32[31,256]{1,0:T(8,128)S(1)}, f32[31,256]{1,0:T(8,128)}, u32[]{:S(2)}) copy-start(f32[31,256]{1,0:T(8,128)} %at_ref.1) | copy-start | bytes 95236
  0.0 1.1 %copy-start.1 = (f32[31,256]{1,0:T(8,128)S(1)}, f32[31,256]{1,0:T(8,128)}, u32[]{:S(2)}) copy-start(f32[31,256]{1,0:T(8,128)} %rt_ref.1) | copy-start | bytes 95236
  0.0 1.1 %copy-start.2 = (bf16[64,256]{1,0:T(8,128)(2,1)S(1)}, bf16[64,256]{1,0:T(8,128)(2,1)}, u32[]{:S(2)}) copy-start(bf16[64,256]{1,0:T(8,128)(2,1)} %wi_ref.1) | copy-start | bytes 98308
  0.0 1.1 %copy-start.3 = (bf16[64,256]{1,0:T(8,128)(2,1)S(1)}, bf16[64,256]{1,0:T(8,128)(2,1)}, u32[]{:S(2)}) copy-start(bf16[64,256]{1,0:T(8,128)(2,1)} %wo_ref.1) | copy-start | bytes 98308
  0.0 1.1 %copy-start.4 = (f32[256]{0:T(256)S(1)}, f32[256]{0:T(256)}, u32[]{:S(2)}) copy-start(f32[256]{0:T(256)} %param.14) | copy-start | bytes 3076
  0.0 1.1 %copy-start.5 = (f32[256]{0:T(256)S(1)}, f32[256]{0:T(256)}, u32[]{:S(2)}) copy-start(f32[256]{0:T(256)} %param.15) | copy-start | bytes 3076
  0.0 1.1 %copy-start.6 = (f32[256]{0:T(256)S(1)}, f32[256]{0:T(256)}, u32[]{:S(2)}) copy-start(f32[256]{0:T(256)} %param.16) | copy-start | bytes 3076
  0.0 1.1 %copy-start.7 = (f32[256]{0:T(256)S(1)}, f32[256]{0:T(256)}, u32[]{:S(2)}) copy-start(f32[256]{0:T(256)} %param.20) | copy-start | bytes 3076
  0.1 1.1 %copy-start.8 = (f32[256]{0:T(256)S(1)}, f32[256]{0:T(256)}, u32[]{:S(2)}) copy-start(f32[256]{0:T(256)} %param.21) | copy-start | bytes 3076
  0.1 1.1 %copy-start.9 = (bf16[64]{0:T(256)(128)(2,1)S(1)}, bf16[64]{0:T(256)(128)(2,1)}, u32[]{:S(2)}) copy-start(bf16[64]{0:T(256)(128)(2,1)} %param.18) | copy-start | bytes 388

commit v4 on v3

--- a/solution.py
+++ b/solution.py
@@ -121,6 +121,7 @@
 
     lax.fori_loop(1, outer, own_outer, 0)
     to_inner(mine + my_slot)
+    to_inner(theirs + my_slot)
     piece_copy(mine + my_slot, grp, sibling).start()
     piece_copy(theirs + my_slot, grp, sibling).start()
 
@@ -147,6 +148,17 @@
         return c
 
     lax.fori_loop(1, outer, from_outer, 0)
+
+    def from_inner(i, c, swap=True):
+        for j in range(1, inner):
+            piece = mine + base + chip_of(ring(i, outer, my_z), ring(j, inner, my_y))
+            piece_copy(piece, grp, sibling).wait_recv()
+            if swap:
+                piece_copy(piece, 1 - grp, me).start()
+            piece_copy(piece, grp, sibling).start()
+        return c
+
+    from_inner(0, 0, swap=False)
 
     def pairs(s, c):
         v = recv1[s].astype(F32).reshape(al, 8, channels)
@@ -185,15 +197,7 @@
     lax.fori_loop(1, n, exchange2, 0)
     recv2[me] = send2[me]
 
-    def from_inner(i, c):
-        for j in range(1, inner):
-            piece = mine + base + chip_of(ring(i, outer, my_z), ring(j, inner, my_y))
-            piece_copy(piece, grp, sibling).wait_recv()
-            piece_copy(piece, 1 - grp, me).start()
-            piece_copy(piece, grp, sibling).start()
-        return c
-
-    lax.fori_loop(0, outer, from_inner, 0)
+    lax.fori_loop(1, outer, from_inner, 0)
 
     def from_group(i, c):
         piece = theirs + base + ring(i, chips, my_chip)
@@ -201,7 +205,6 @@
         piece_copy(piece, grp, sibling).start()
         return c
 
-    lax.fori_loop(1, chips, from_group, 0)
 
     arrived3 = bias.at[pl.ds(0, n - 1)]
     pltpu.make_async_copy(arrived3, arrived3, br_sem).wait()
@@ -254,6 +257,7 @@
         o_ref[at, :] = (x_ref[at, :].astype(F32) + branch.astype(F32)).astype(BF16)
         return c
 
+    lax.fori_loop(1, chips, from_group, 0)
     mlp(0, 0, True)
     if n // block > 1:
         lax.fori_loop(1, n // block, lambda b, c: mlp(b, c, False), 0)

time: 23.2 us -> 23.2 us (level)
  no operation moved by 1% of the time
where the time goes in v4:
time: 23.2 us; the launch traced here: 23.1 us
  Pallas kernels  21.2 us (91%)
  local copies, waits for them, and re-layouts  1.75 us (8%)
    pallas_call x1, Pallas kernels, local(): pl.pallas_call(functools.partial(kernel, n, inner, taps, al, hl), out_sha...  21.2 us
    reshape x1, local copies, waits for them, and re-layouts, local(): flat = features.reshape(axial * 8, channels)  1.02 us
    reshape x1, local copies, waits for them, and re-layouts, local(): return out.reshape(features.shape)  0.69 us

profile of v4, /device:TPU:1, one launch (start us, length us, event | category | flops | bytes accessed | tf_op | source)
XLA Modules:
  0.0 23.1 jit_solution(11955878381893278021)
XLA Ops:
  0.0 0.0 copy-start
  0.0 0.0 copy-start.1
  0.0 0.0 copy-start.2
  0.0 0.0 copy-start.3
  0.0 0.0 copy-start.4
  0.0 0.0 copy-start.5
  0.0 0.0 copy-start.6
  0.0 0.0 copy-start.7
  0.1 0.0 copy-start.8
  0.1 0.0 copy-start.9
  0.1 1.0 %reshape.24.x_ref = bf16[256,256]{1,0:T(8,128)(2,1)S(1)} reshape(bf16[32,2,4,256]{3,2,1,0:T(4,128)(2,1)} %param.11) | data formatting | bytes 262144 | tf_op jit(solution)/shard_map/reshape | solution.py:298
  1.1 0.0 copy-done
  1.1 0.0 copy-done.1
  1.1 0.0 copy-done.2
  1.1 0.0 copy-done.3
  1.1 0.0 copy-done.4
  1.1 0.0 copy-done.5
  1.2 0.0 copy-done.6
  1.2 0.0 copy-done.7
  1.2 0.0 copy-done.8
  1.2 0.0 copy-done.9
  1.2 21.2 %shard_map.109 = bf16[256,256]{1,0:T(8,128)(2,1)S(1)} custom-call(bf16[256,256]{1,0:T(8,128)(2,1)S(1)} %reshape.24.x_ref, f32[31,256]{1,0:T(8,128)S(1)} %copy-done, f32[31,256]{1,0:T(8,128)S(1)} %copy-done.1, f32[1,256]{1,0:T(1,128)S(1)} %bitcast.6, f32[1,256]{1,0:T(1,128)S(1)} %bitcast.7, f32[1,256]{1,0:T(1,128)S(1)} %bitcast.8, ...), custom_call_target="tpu_custom_call" | custom-call | flops 276561920 | bytes 1310720 | tf_op jit(solution)/shard_map/pallas_call | solution.py:305
  22.4 0.7 %reshape.31 = bf16[32,2,4,256]{3,2,1,0:T(4,128)(2,1)} reshape(bf16[256,256]{1,0:T(8,128)(2,1)S(1)} %shard_map.109) | data formatting | bytes 262144 | tf_op jit(solution)/shard_map/reshape | solution.py:336
Async XLA Ops:
  0.0 1.1 %copy-start = (f32[31,256]{1,0:T(8,128)S(1)}, f32[31,256]{1,0:T(8,128)}, u32[]{:S(2)}) copy-start(f32[31,256]{1,0:T(8,128)} %at_ref.1) | copy-start | bytes 95236
  0.0 1.1 %copy-start.1 = (f32[31,256]{1,0:T(8,128)S(1)}, f32[31,256]{1,0:T(8,128)}, u32[]{:S(2)}) copy-start(f32[31,256]{1,0:T(8,128)} %rt_ref.1) | copy-start | bytes 95236
  0.0 1.1 %copy-start.2 = (bf16[64,256]{1,0:T(8,128)(2,1)S(1)}, bf16[64,256]{1,0:T(8,128)(2,1)}, u32[]{:S(2)}) copy-start(bf16[64,256]{1,0:T(8,128)(2,1)} %wi_ref.1) | copy-start | bytes 98308
  0.0 1.1 %copy-start.3 = (bf16[64,256]{1,0:T(8,128)(2,1)S(1)}, bf16[64,256]{1,0:T(8,128)(2,1)}, u32[]{:S(2)}) copy-start(bf16[64,256]{1,0:T(8,128)(2,1)} %wo_ref.1) | copy-start | bytes 98308
  0.0 1.1 %copy-start.4 = (f32[256]{0:T(256)S(1)}, f32[256]{0:T(256)}, u32[]{:S(2)}) copy-start(f32[256]{0:T(256)} %param.14) | copy-start | bytes 3076
  0.0 1.1 %copy-start.5 = (f32[256]{0:T(256)S(1)}, f32[256]{0:T(256)}, u32[]{:S(2)}) copy-start(f32[256]{0:T(256)} %param.15) | copy-start | bytes 3076
  0.0 1.1 %copy-start.6 = (f32[256]{0:T(256)S(1)}, f32[256]{0:T(256)}, u32[]{:S(2)}) copy-start(f32[256]{0:T(256)} %param.16) | copy-start | bytes 3076
  0.0 1.1 %copy-start.7 = (f32[256]{0:T(256)S(1)}, f32[256]{0:T(256)}, u32[]{:S(2)}) copy-start(f32[256]{0:T(256)} %param.20) | copy-start | bytes 3076
  0.1 1.1 %copy-start.8 = (f32[256]{0:T(256)S(1)}, f32[256]{0:T(256)}, u32[]{:S(2)}) copy-start(f32[256]{0:T(256)} %param.21) | copy-start | bytes 3076
  0.1 1.1 %copy-start.9 = (bf16[64]{0:T(256)(128)(2,1)S(1)}, bf16[64]{0:T(256)(128)(2,1)}, u32[]{:S(2)}) copy-start(bf16[64]{0:T(256)(128)(2,1)} %param.18) | copy-start | bytes 388
